TPU v7x, 32 devices: a whole 2x2x4 slice. The times are simulated.
32 devices in a mesh: scene: 2 (over x), aperture: 16 (over z, y, core).
Axes of the slice: x: 2, y: 2, z: 4, core: 2. Of those that a mesh axis runs over, the one named last changes fastest.
Arguments:
- subimages: bfloat16 [32, 2, 32, 16384], P(('scene', 'aperture')), parts along dimension 0, may hold values from -6 to 6
- range_shift: int32 [32], P(('scene', 'aperture')), parts along dimension 0, may hold values from 0 to 63, as said below
- interp_weights: bfloat16 [3, 32, 2, 64, 8], P(None, 'scene'), parts along dimension 1, may hold values from -1.5 to 1.5
- band_start: int32 [3, 32, 64], P(None, 'scene'), parts along dimension 1, may hold values from 0 to 24
- phase_params: float32 [3, 32, 2], P(None, 'scene'), parts along dimension 1, may hold values from -6 to 6
- block_owner: int32 [32], P('scene'), parts along dimension 0, may hold values from 0 to 15, each once
- group_phase: float32 [32, 2, 1024], P(('scene', 'aperture')), parts along dimension 0, may hold values from -3.140625 to 3.140625
Outputs:
- final_image: bfloat16 [32, 2, 32, 8, 1024], P(('scene', 'aperture')), parts along dimension 0
There are 2 independent parts, one for each index of `scene`. A program takes and returns all parts, laid end to end along the dimension named above; each array names one. Nothing has to cross between parts.
Inputs may be any that keep to these rules, and one draw needn't show every extreme that they name: `range_shift`: some subimage has the offset 64 - 1. `band_start`: a band lies within the input beams. `block_owner`: each range block is held by exactly one device.
All inputs are finite; a program needn't handle non-finite values.
Results may differ from a plain program's by a relative error of at most 0.0064.
Values may be sent and summed in bfloat16 or wider, within the bound.
A program may use at most 64 MiB of HBM per device.

v0:
```python
import jax
import jax.numpy as jnp
from jax import lax
from jax.sharding import PartitionSpec as P

SECTIONS = 3
MAXOFF = 64


HALF_ROOT = 0.7071067811865476


def swapped(shard, axis, stride):
    return lax.ppermute(shard, axis, [(i, i ^ 1 << stride) for i in range(lax.axis_size(axis))])


def band_matrix(tap_weights, tap_starts, columns):
    column_ids = jnp.arange(columns, dtype=jnp.int32)
    tap_ids = jnp.arange(tap_weights.shape[-1], dtype=jnp.int32)
    targets = tap_starts[:, None] + tap_ids[None, :]
    hits = targets[:, :, None] == column_ids[None, None, :]
    return jnp.sum(
        jnp.where(hits[None], tap_weights[:, :, :, None], jnp.zeros((), tap_weights.dtype)), axis=2
    )


def stacked_operator(band_dense):
    upper = jnp.concatenate([band_dense[0], -band_dense[1]], axis=1)
    lower = jnp.concatenate([band_dense[1], band_dense[0]], axis=1)
    return jnp.concatenate([upper, lower], axis=0)


def turn_at(values, params, positions):
    phase_angle = params[0] * positions + params[1]
    cosine = jnp.cos(phase_angle)
    sine_part = jnp.sin(phase_angle)
    return jnp.stack(
        [values[0] * cosine - values[1] * sine_part, values[0] * sine_part + values[1] * cosine]
    )


def phase_turn(values, params, range_count):
    positions = jnp.arange(range_count, dtype=jnp.float32) / range_count
    return turn_at(values, params, positions)


def project_rows(row_weights, row_starts, params, image):
    beam_count = image.shape[1]
    range_count = image.shape[2]
    row_count = row_weights.shape[1]
    block_matrix = stacked_operator(band_matrix(row_weights, row_starts, beam_count))
    product = jnp.dot(
        block_matrix, image.reshape(2 * beam_count, range_count), preferred_element_type=jnp.float32
    )
    return phase_turn(product.reshape(2, row_count, range_count), params, range_count)


def combine_groups(pieces, group_phase, groups):
    cosine = jnp.cos(group_phase[0])[:, None, None, :]
    sine_part = jnp.sin(group_phase[0])[:, None, None, :]
    real_part = jnp.sum(pieces[:, :, 0] * cosine - pieces[:, :, 1] * sine_part, axis=0)
    imag_part = jnp.sum(pieces[:, :, 0] * sine_part + pieces[:, :, 1] * cosine, axis=0)
    result = jnp.stack([real_part, imag_part]) * (1.0 / groups**0.5)
    return jnp.transpose(result, (0, 2, 1, 3))[None].astype(jnp.bfloat16)


def shards(
    subimages, range_shift, interp_weights, band_start, phase_params, block_owner, group_phase
):
    local_image = subimages[0]
    beam_count = local_image.shape[1]
    range_count = local_image.shape[2]
    padded = jnp.pad(local_image, ((0, 0), (0, 0), (MAXOFF, 0)))
    image = lax.dynamic_slice_in_dim(padded, MAXOFF - range_shift[0], range_count, 2)
    position = lax.axis_index("aperture")
    device_count = lax.axis_size("aperture")
    sectors = 2**SECTIONS
    groups = group_phase.shape[1]
    block = range_count // device_count
    for level in range(SECTIONS):
        which_half = jnp.bitwise_and(jnp.right_shift(position, level), 1)
        local_weights = interp_weights[level][position]
        local_starts = band_start[level][position]
        local_params = phase_params[level][position]
        full_rows = project_rows(local_weights, local_starts, local_params, image)
        kept_rows = lax.dynamic_slice_in_dim(full_rows, which_half * beam_count, beam_count, 1)
        other_rows = lax.dynamic_slice_in_dim(
            full_rows, (1 - which_half) * beam_count, beam_count, 1
        )
        received = swapped(other_rows, "aperture", level)
        image = ((kept_rows + received) * HALF_ROOT).astype(jnp.bfloat16)
    blocks = image.reshape(2, beam_count, device_count, block)
    outgoing = jnp.take(blocks, block_owner, axis=2)
    received_blocks = lax.all_to_all(outgoing, "aperture", split_axis=2, concat_axis=2, tiled=True)
    pieces = jnp.transpose(
        received_blocks.reshape(2, beam_count, groups, sectors, block), (2, 3, 0, 1, 4)
    ).astype(jnp.float32)
    return combine_groups(pieces, group_phase, groups)


def solution(mesh):
    placed = (
        P(("scene", "aperture"), None, None, None),
        P(("scene", "aperture")),
        P(None, "scene", None, None, None),
        P(None, "scene", None),
        P(None, "scene", None),
        P("scene"),
        P(("scene", "aperture"), None, None),
    )
    return jax.shard_map(
        shards,
        mesh=mesh,
        in_specs=placed,
        out_specs=P(("scene", "aperture"), None, None, None, None),
        check_vma=False,
    )
```

profile of v0, /device:TPU:9, one launch (start us, length us, event | category | flops | bytes accessed | tf_op | source)
XLA Modules:
  0.0 293.5 jit_solution(18327888882667539921)
XLA Ops:
  3.8 2.2 pad_dynamic-slice_fusion.12
  7.5 1.3 fusion.39
  8.9 1.1 add_bitcast_fusion.2
  10.0 2.4 fusion.10
  13.3 1.2 copy-done.1
  18.4 3.9 %collective-permute-done = f32[2,32,16384]{2,1,0:T(8,128)} collective-permute-done((f32[2,32,16384]{2,1,0:T(8,128)}, f32[2,32,16384]{2,1,0:T(8,128)}, u32[]{:S(2)}, u32[]{:S(2)}) %collective-permute-start) | collective-permute-done | bytes 4194336 | tf_op jit(solution)/shard_map/ppermute | solution.py:14
  22.3 3.9 %fusion.14 = bf16[2,32,16384]{2,1,0:T(8,128)(2,1)S(1)} fusion(f32[2,32,16384]{2,1,0:T(8,128)} %collective-permute-done, s32[]{:T(128)S(6)} %select_n.57, f32[1,64,16384]{2,1,0:T(8,128)} %copy-done.1, f32[1,64,16384]{2,1,0:T(8,128)} %copy-done), kind=kLoop, calls=%fused_computation.27 | loop fusion | flops 4194304 | bytes 14680068 | tf_op jit(solution)/shard_map/convert_element_type | solution.py:91
  26.2 1.3 fusion.31
  28.7 2.4 fusion.5
  31.9 1.2 copy-done.3
  33.1 1.2 collective-permute-start.1
  37.4 87.8 %collective-permute-done.1 = f32[2,32,16384]{2,1,0:T(8,128)} collective-permute-done((f32[2,32,16384]{2,1,0:T(8,128)}, f32[2,32,16384]{2,1,0:T(8,128)}, u32[]{:S(2)}, u32[]{:S(2)}) %collective-permute-start.1) | collective-permute-done | bytes 4194336 | tf_op jit(solution)/shard_map/ppermute | solution.py:14
  125.2 3.9 %fusion.9 = bf16[2,32,16384]{2,1,0:T(8,128)(2,1)S(1)} fusion(f32[2,32,16384]{2,1,0:T(8,128)} %collective-permute-done.1, s32[]{:T(128)S(6)} %select_n.59, f32[1,64,16384]{2,1,0:T(8,128)} %copy-done.3, f32[1,64,16384]{2,1,0:T(8,128)} %copy-done.2), kind=kLoop, calls=%fused_computation.22 | loop fusion | flops 4194304 | bytes 14680068 | tf_op jit(solution)/shard_map/convert_element_type | solution.py:91
  129.1 1.4 fusion.23
  131.6 2.4 fusion
  134.8 1.2 copy-done.5
  136.3 90.9 %collective-permute-done.2 = f32[2,32,16384]{2,1,0:T(8,128)} collective-permute-done((f32[2,32,16384]{2,1,0:T(8,128)}, f32[2,32,16384]{2,1,0:T(8,128)}, u32[]{:S(2)}, u32[]{:S(2)}) %collective-permute-start.2) | collective-permute-done | bytes 4194336 | tf_op jit(solution)/shard_map/ppermute | solution.py:14
  227.2 3.9 %fusion.4 = bf16[2,32,16384]{2,1,0:T(8,128)(2,1)S(1)} fusion(f32[2,32,16384]{2,1,0:T(8,128)} %collective-permute-done.2, s32[]{:T(128)S(6)} %select_n.61, f32[1,64,16384]{2,1,0:T(8,128)} %copy-done.5, f32[1,64,16384]{2,1,0:T(8,128)} %copy-done.4), kind=kLoop, calls=%fused_computation.17 | loop fusion | flops 4194304 | bytes 14680068 | tf_op jit(solution)/shard_map/convert_element_type | solution.py:91
  231.0 1.5 copy.25
  232.6 2.3 gather_fusion
  234.8 1.6 select_bitcast_fusion
  236.4 8.1 %all-to-all-start = ((bf16[2,32,16,1024]{3,1,0,2:T(8,128)(2,1)}), bf16[2,32,16,1024]{3,1,0,2:T(8,128)(2,1)S(1)}, u32[]{:S(2)}, u32[]{:S(2)}) async-start(bf16[2,32,16,1024]{3,1,0,2:T(8,128)(2,1)} %select_bitcast_fusion), calls=%async_computation | async-start | bytes 4194304 | tf_op jit(solution)/shard_map/all_to_all | solution.py:94
  244.7 45.8 %all-to-all-done = bf16[2,32,16,1024]{3,1,0,2:T(8,128)(2,1)S(1)} async-done(((bf16[2,32,16,1024]{3,1,0,2:T(8,128)(2,1)}), bf16[2,32,16,1024]{3,1,0,2:T(8,128)(2,1)S(1)}, u32[]{:S(2)}, u32[]{:S(2)}) %all-to-all-start) | async-done | bytes 2097184 | tf_op jit(solution)/shard_map/all_to_all | solution.py:94
  292.0 1.5 copy.21
  (56 shorter events, 16.2 us)
Async XLA Ops:
  10.0 3.2 %copy-start = (f32[1,64,16384]{2,1,0:T(8,128)}, f32[1,64,16384]{2,1,0:T(8,128)S(1)}, u32[]{:S(2)}) copy-start(f32[1,64,16384]{2,1,0:T(8,128)S(1)} %get-tuple-element.11) | copy-start | bytes 12582916
  10.0 4.5 %copy-start.1 = (f32[1,64,16384]{2,1,0:T(8,128)}, f32[1,64,16384]{2,1,0:T(8,128)S(1)}, u32[]{:S(2)}) copy-start(f32[1,64,16384]{2,1,0:T(8,128)S(1)} %get-tuple-element.12) | copy-start | bytes 12582916
  14.5 7.8 %collective-permute-start = (f32[2,32,16384]{2,1,0:T(8,128)}, f32[2,32,16384]{2,1,0:T(8,128)}, u32[]{:S(2)}, u32[]{:S(2)}) collective-permute-start(f32[2,32,16384]{2,1,0:T(8,128)} %fusion.10), channel_id=1, source_target_pairs={{0,1},{1,0},{2,3},{3,2},{4,5},{5,4},{6,7},{7,6},{8,9},{9,8},{10,11... | collective-permute-start | bytes 12582920 | tf_op jit(solution)/shard_map/ppermute | solution.py:14
  28.6 3.2 %copy-start.2 = (f32[1,64,16384]{2,1,0:T(8,128)}, f32[1,64,16384]{2,1,0:T(8,128)S(1)}, u32[]{:S(2)}) copy-start(f32[1,64,16384]{2,1,0:T(8,128)S(1)} %get-tuple-element.9) | copy-start | bytes 12582916
  28.7 4.5 %copy-start.3 = (f32[1,64,16384]{2,1,0:T(8,128)}, f32[1,64,16384]{2,1,0:T(8,128)S(1)}, u32[]{:S(2)}) copy-start(f32[1,64,16384]{2,1,0:T(8,128)S(1)} %get-tuple-element.10) | copy-start | bytes 12582916
  33.1 92.1 %collective-permute-start.1 = (f32[2,32,16384]{2,1,0:T(8,128)}, f32[2,32,16384]{2,1,0:T(8,128)}, u32[]{:S(2)}, u32[]{:S(2)}) collective-permute-start(f32[2,32,16384]{2,1,0:T(8,128)} %fusion.5), channel_id=1, source_target_pairs={{0,2},{1,3},{2,0},{3,1},{4,6},{5,7},{6,4},{7,5},{8,10},{9,11},{10,... | collective-permute-start | bytes 12582920 | tf_op jit(solution)/shard_map/ppermute | solution.py:14
  131.5 3.2 %copy-start.4 = (f32[1,64,16384]{2,1,0:T(8,128)}, f32[1,64,16384]{2,1,0:T(8,128)S(1)}, u32[]{:S(2)}) copy-start(f32[1,64,16384]{2,1,0:T(8,128)S(1)} %get-tuple-element.7) | copy-start | bytes 12582916
  131.5 4.5 %copy-start.5 = (f32[1,64,16384]{2,1,0:T(8,128)}, f32[1,64,16384]{2,1,0:T(8,128)S(1)}, u32[]{:S(2)}) copy-start(f32[1,64,16384]{2,1,0:T(8,128)S(1)} %get-tuple-element.8) | copy-start | bytes 12582916
  131.6 4.7 %copy-start.7 = (s32[16]{0:T(128)S(1)}, s32[16]{0:T(128)}, u32[]{:S(2)}) copy-start(s32[16]{0:T(128)} %param.12) | copy-start | bytes 196
  136.0 91.2 %collective-permute-start.2 = (f32[2,32,16384]{2,1,0:T(8,128)}, f32[2,32,16384]{2,1,0:T(8,128)}, u32[]{:S(2)}, u32[]{:S(2)}) collective-permute-start(f32[2,32,16384]{2,1,0:T(8,128)} %fusion), channel_id=1, source_target_pairs={{0,4},{1,5},{2,6},{3,7},{4,0},{5,1},{6,2},{7,3},{8,12},{9,13},{10,... | collective-permute-start | bytes 12582920 | tf_op jit(solution)/shard_map/ppermute | solution.py:14
  234.8 9.7 %copy-start.6 = (f32[1,2,1024]{2,1,0:T(2,128)S(1)}, f32[1,2,1024]{2,1,0:T(2,128)}, u32[]{:S(2)}) copy-start(f32[1,2,1024]{2,1,0:T(2,128)} %param.13) | copy-start | bytes 24580
  236.4 54.1 %all-to-all-start = ((bf16[2,32,16,1024]{3,1,0,2:T(8,128)(2,1)}), bf16[2,32,16,1024]{3,1,0,2:T(8,128)(2,1)S(1)}, u32[]{:S(2)}, u32[]{:S(2)}) async-start(bf16[2,32,16,1024]{3,1,0,2:T(8,128)(2,1)} %select_bitcast_fusion), calls=%async_computation | async-start | bytes 4194304 | tf_op jit(solution)/shard_map/all_to_all | solution.py:94
where the time goes:
time: 295 us; the launch traced here: 294 us
  waiting for transfers between devices  228 us (77%)
  other arithmetic  29.8 us (10%)
  local copies, waits for them, and re-layouts  18.1 us (6%)
  starting transfers between devices  10.3 us (3%)
  matrix products  4.05 us (1%)
    ppermute x3, waiting for transfers between devices, swapped(): lax.ppermute(shard, axis, [(i, i ^ 1 << stride) for i in range(lax.axis_s...  183 us
    all_to_all x1, waiting for transfers between devices, shards(): lax.all_to_all(outgoing, 'aperture', split_axis=2, concat_axis=2, tiled=T...  45.8 us
    convert_element_type x3, other arithmetic, shards(): image = ((kept_rows + received) * HALF_ROOT).astype(jnp.bfloat16)  11.6 us
    another operation x6, other arithmetic, turn_at(): jnp.stack([values[0] * cosine - values[1] * sine_part, values[0] * sine_p...  10.5 us
    all_to_all x1, starting transfers between devices, shards(): lax.all_to_all(outgoing, 'aperture', split_axis=2, concat_axis=2, tiled=T...  8.09 us
    unnamed x16, local copies, waits for them, and re-layouts  6.17 us
  transfers between devices with their start and end apart: 4, of which 4 were waited for; matrix products, arithmetic and copies ran while one was open for 2% of the time, Pallas kernels for 0%

commit v1 on v0

v1 whole, which is shorter than its diff:
```python
import jax
import jax.numpy as jnp
from jax import lax
from jax.sharding import PartitionSpec as P

SECTIONS = 3
MAXOFF = 64
HALF_ROOT = 0.7071067811865476


def band_matrices(weights, starts, columns):
    column_ids = jnp.arange(columns, dtype=jnp.int32)
    tap_ids = jnp.arange(weights.shape[-1], dtype=jnp.int32)
    targets = starts[..., None] + tap_ids
    hits = targets[..., None] == column_ids
    dense = jnp.sum(
        jnp.where(hits[:, None], weights[..., None], jnp.zeros((), weights.dtype)), axis=3
    )
    upper = jnp.concatenate([dense[:, 0], -dense[:, 1]], axis=2)
    lower = jnp.concatenate([dense[:, 1], dense[:, 0]], axis=2)
    return jnp.concatenate([upper, lower], axis=1)


def shards(
    subimages, range_shift, interp_weights, band_start, phase_params, block_owner, group_phase
):
    local_image = subimages[0]
    beams = local_image.shape[1]
    range_count = local_image.shape[2]
    count = lax.axis_size("aperture")
    me = lax.axis_index("aperture")
    block = range_count // count
    groups = group_phase.shape[1]
    sectors = 2**SECTIONS
    padded = jnp.pad(local_image, ((0, 0), (0, 0), (MAXOFF, 0)))
    image = lax.dynamic_slice_in_dim(padded, MAXOFF - range_shift[0], range_count, 2)
    blocks = image.reshape(2, beams, count, block)
    outgoing = jnp.transpose(jnp.take(blocks, block_owner, axis=2), (2, 0, 1, 3))
    images = lax.all_to_all(outgoing, "aperture", split_axis=0, concat_axis=0, tiled=True)
    first = block_owner[me] * block
    positions = (first + jnp.arange(block, dtype=jnp.int32)).astype(jnp.float32) / range_count
    for level in range(SECTIONS):
        operator = band_matrices(interp_weights[level], band_start[level], beams)
        product = jnp.einsum(
            "pjk,pkr->pjr",
            operator,
            images.reshape(count, 2 * beams, block),
            preferred_element_type=jnp.float32,
        ).reshape(count, 2, 2 * beams, block)
        angle = phase_params[level][:, 0:1] * positions + phase_params[level][:, 1:2]
        cosine = jnp.cos(angle)[:, None]
        sine = jnp.sin(angle)[:, None]
        real = product[:, 0] * cosine - product[:, 1] * sine
        imag = product[:, 0] * sine + product[:, 1] * cosine
        turned = jnp.stack([real, imag], axis=1)
        step = 1 << level
        pairs = turned.reshape(count // (2 * step), 2, step, 2, 2, beams, block)
        merged = ((pairs[:, 0] + pairs[:, 1]) * HALF_ROOT).astype(jnp.bfloat16)
        images = jnp.transpose(merged, (0, 3, 1, 2, 4, 5)).reshape(count, 2, beams, block)
    pieces = images.astype(jnp.float32).reshape(groups, sectors, 2, beams, block)
    cosine = jnp.cos(group_phase[0])[:, None, None, :]
    sine = jnp.sin(group_phase[0])[:, None, None, :]
    real = jnp.sum(pieces[:, :, 0] * cosine - pieces[:, :, 1] * sine, axis=0)
    imag = jnp.sum(pieces[:, :, 0] * sine + pieces[:, :, 1] * cosine, axis=0)
    result = jnp.stack([real, imag]) * (1.0 / groups**0.5)
    return jnp.transpose(result, (0, 2, 1, 3))[None].astype(jnp.bfloat16)


def solution(mesh):
    placed = (
        P(("scene", "aperture"), None, None, None),
        P(("scene", "aperture")),
        P(None, "scene", None, None, None),
        P(None, "scene", None),
        P(None, "scene", None),
        P("scene"),
        P(("scene", "aperture"), None, None),
    )
    return jax.shard_map(
        shards,
        mesh=mesh,
        in_specs=placed,
        out_specs=P(("scene", "aperture"), None, None, None, None),
        check_vma=False,
    )
```

time: 295 us -> 83.9 us (0.28)
  waiting for transfers between devices: 228 us -> 39.8 us
  local copies, waits for them, and re-layouts: 18.1 us -> 7.35 us
  other arithmetic: 29.8 us -> 21.6 us
  starting transfers between devices: 10.3 us -> 6.61 us
    ppermute x3 -> x0, waiting for transfers between devices: 183 us -> none  [swapped(): lax.ppermute(shard, axis, [(i, i ^ 1 << stride) for i in range(lax.axis_s...]
    convert_element_type x5 -> x4, other arithmetic: 12.3 us -> 3.54 us  [the longest x2 2.26 us: shards(): merged = ((pairs[:, 0] + pairs[:, 1]) * HALF_ROOT).astype(jnp.bfloat16)]
    another operation x6 -> x2, other arithmetic: 10.5 us -> 2.04 us  [shards(): turned = jnp.stack([real, imag], axis=1)]
    sub x0 -> x3, other arithmetic: none -> 6.25 us  [shards(): real = product[:, 0] * cosine - product[:, 1] * sine]
    unnamed x16 -> x14, local copies, waits for them, and re-layouts: 6.17 us -> 0.03 us
    all_to_all x1, waiting for transfers between devices: 45.8 us -> 39.8 us  [shards(): lax.all_to_all(outgoing, 'aperture', split_axis=0, concat_axis=0, tiled=T...]
    slice x6 -> x0, local copies, waits for them, and re-layouts: 4.13 us -> none  [the longest x3 1.76 us: turn_at(): phase_angle = params[0] * positions + params[1]]
  transfers between devices with their start and end apart: 4 -> 1, of which waited for: 4 -> 1; matrix products, arithmetic and copies ran while one was open for 2% -> 7% of each run, Pallas kernels for 0% -> 0%
where the time goes in v1:
time: 83.9 us; the launch traced here: 82.2 us
  waiting for transfers between devices  39.8 us (47%)
  other arithmetic  21.6 us (26%)
  local copies, waits for them, and re-layouts  7.35 us (9%)
  starting transfers between devices  6.61 us (8%)
  matrix products  5.23 us (6%)
  between operations  1.64 us (2%)
    all_to_all x1, waiting for transfers between devices, shards(): lax.all_to_all(outgoing, 'aperture', split_axis=0, concat_axis=0, tiled=T...  39.8 us
    all_to_all x1, starting transfers between devices, shards(): lax.all_to_all(outgoing, 'aperture', split_axis=0, concat_axis=0, tiled=T...  6.61 us
    sub x3, other arithmetic, shards(): real = product[:, 0] * cosine - product[:, 1] * sine  6.25 us
    dot_general x3, matrix products, shards(): jnp.einsum('pjk,pkr->pjr', operator, images.reshape(count, 2 * beams, blo...  5.23 us
    select_n x2, other arithmetic, shards(): jnp.take(blocks, block_owner, axis=2)  3.91 us
    convert_element_type x2, other arithmetic, shards(): merged = ((pairs[:, 0] + pairs[:, 1]) * HALF_ROOT).astype(jnp.bfloat16)  2.26 us
    dynamic_slice x1, local copies, waits for them, and re-layouts, shards(): lax.dynamic_slice_in_dim(padded, MAXOFF - range_shift[0], range_count, 2)  2.21 us
    reduce_sum x3, other arithmetic, band_matrices(): jnp.sum(jnp.where(hits[:, None], weights[..., None], jnp.zeros((), weight...  2.08 us
  transfers between devices with their start and end apart: 1, of which 1 were waited for; matrix products, arithmetic and copies ran while one was open for 7% of the time, Pallas kernels for 0%

profile of v1, /device:TPU:9, one launch (start us, length us, event | category | flops | bytes accessed | tf_op | source)
XLA Modules:
  0.0 82.2 jit_solution(4805531863298169561)
XLA Ops:
  0.0 0.7 compare_select_fusion
  0.7 0.7 compare_and_fusion
  2.0 2.2 %pad_dynamic-slice_fusion = bf16[2,32,16384]{2,1,0:T(8,128)(2,1)S(1)} fusion(s32[]{:T(128)S(6)} %select_n.33, bf16[2,32,16384]{2,1,0:T(8,128)(2,1)} %bitcast.150), kind=kLoop, calls=%fused_computation.31 | loop fusion | bytes 4194308 | tf_op jit(solution)/shard_map/dynamic_slice | solution.py:36
  4.4 2.0 %gather_fusion = bf16[16,2,32,1024]{3,2,1,0:T(8,128)(2,1)} fusion(bf16[2,32,16,1024]{3,1,2,0:T(8,128)(2,1)S(1)} %bitcast.145, s32[1024]{0:T(1024)S(1)} %pad_clamp_fusion), kind=kCustom, calls=%fused_computation | custom fusion | bytes 4194368 | tf_op jit(solution)/shard_map/jit(_take)/gather | solution.py:38
  6.4 3.3 %broadcast_select_fusion = bf16[16,2,32,1024]{3,2,1,0:T(8,128)(2,1)} fusion(bf16[16,2,32,1024]{3,2,1,0:T(8,128)(2,1)} %gather_fusion, pred[16]{0:T(512)(128)(4,1)S(1)} %compare_and_fusion), kind=kLoop, calls=%fused_computation.45 | loop fusion | flops 1048576 | bytes 4194320 | tf_op jit(solution)/shard_map/jit(_take)/select_n | solution.py:38
  9.7 6.6 %all-to-all-start = ((bf16[16,2,32,1024]{3,2,1,0:T(8,128)(2,1)}), bf16[16,2,32,1024]{3,2,1,0:T(8,128)(2,1)S(1)}, u32[]{:S(2)}, u32[]{:S(2)}) async-start(bf16[16,2,32,1024]{3,2,1,0:T(8,128)(2,1)} %broadcast_select_fusion), calls=%async_computation | async-start | bytes 4194304 | tf_op jit(solution)/shard_map/all_to_all | solution.py:39
  18.2 0.7 select_reduce_fusion
  19.2 0.7 select_reduce_fusion.1
  20.3 0.7 select_reduce_fusion.2
  21.1 1.4 %fusion.37 = (f32[16,1024]{1,0:T(8,128)S(1)}, f32[16,1024]{1,0:T(8,128)S(1)}, f32[16,1024]{1,0:T(8,128)S(1)}, f32[16,1024]{1,0:T(8,128)S(1)}, f32[16,1024]{1,0:T(8,128)}, /*index=5*/f32[16,1024]{1,0:T(8,128)}) fusion(f32[16]{0:T(128)S(1)} %get-tuple-element.45, f32[16]{0:T(128)S(1)} %get-tuple-element.44, f32[1024]{0:T(1024)S(1)} %convert_multiply_fusion, ...), kind=kLoop, calls=%fused_computation.79 | loop fusion | flops 98304 | bytes 397696 | tf_op jit(solution)/shard_map/cos | solution.py:51
  22.5 39.8 %all-to-all-done = bf16[16,2,32,1024]{3,2,1,0:T(8,128)(2,1)S(1)} async-done(((bf16[16,2,32,1024]{3,2,1,0:T(8,128)(2,1)}), bf16[16,2,32,1024]{3,2,1,0:T(8,128)(2,1)S(1)}, u32[]{:S(2)}, u32[]{:S(2)}) %all-to-all-start) | async-done | bytes 2097184 | tf_op jit(solution)/shard_map/all_to_all | solution.py:39
  62.3 1.7 %fusion.28 = f32[16,128,1024]{2,1,0:T(8,128)S(1)} fusion(bf16[16,64,1024]{2,1,0:T(8,128)(2,1)S(1)} %bitcast.147, bf16[16,64,32]{1,2,0:T(8,128)(2,1)S(1)} %get-tuple-element.22, bf16[16,64,32]{1,2,0:T(8,128)(2,1)S(1)} %get-tuple-element.21, bf16[16,64,32]{1,2,0:T(8,128)(2,1)S(1)} %fusion.47), kind=kOutput, calls=%fused_computation.63 | convolution fusion | flops 269484032 | bytes 10682368 | tf_op jit(solution)/shard_map/pjk,pkr->pjr/dot_general | solution.py:44
  64.0 2.1 %multiply_subtract_fusion.2 = (f32[16,1,64,1024]{3,2,1,0:T(8,128)S(1)}, f32[16,1,64,1024]{3,2,1,0:T(8,128)S(1)}) fusion(f32[16,2,64,1024]{3,2,1,0:T(8,128)S(1)} %bitcast.134, f32[16,1024]{1,0:T(8,128)S(1)} %copy-done, f32[16,1024]{1,0:T(8,128)S(1)} %copy-done.1), kind=kLoop, calls=%fused_computation.30 | loop fusion | flops 6291456 | bytes 16908288 | tf_op jit(solution)/shard_map/sub | solution.py:53
  66.1 0.9 %fusion.5 = (f32[8,1,1,2,2,32,1024]{6,5,4,1,0,3,2:T(8,128)S(1)}, f32[8,1,1,2,2,32,1024]{6,5,4,1,0,3,2:T(8,128)S(1)}) fusion(f32[8,2,1,1,2,32,1024]{6,5,4,1,0,3,2:T(8,128)S(1)} %bitcast.139, f32[8,2,1,1,2,32,1024]{6,5,4,1,0,3,2:T(8,128)S(1)} %bitcast.140), kind=kLoop, calls=%fused_computation.12 | loop fusion | flops 2097152 | bytes 16777216 | tf_op jit(solution)/shard_map/stack | solution.py:55
  67.1 1.1 %fusion.9 = bf16[8,1,1,2,2,32,1024]{6,5,3,4,0,2,1:T(8,128)(2,1)S(1)} fusion(f32[8,1,1,2,2,32,1024]{6,5,4,1,0,3,2:T(8,128)S(1)} %get-tuple-element.16, f32[8,1,1,2,2,32,1024]{6,5,4,1,0,3,2:T(8,128)S(1)} %get-tuple-element.15), kind=kLoop, calls=%fused_computation.23 | loop fusion | flops 3145728 | bytes 10485760 | tf_op jit(solution)/shard_map/convert_element_type | solution.py:58
  68.2 1.7 %fusion.20 = f32[16,128,1024]{2,1,0:T(8,128)S(1)} fusion(bf16[16,64,1024]{2,1,0:T(8,128)(2,1)S(1)} %bitcast.143, bf16[16,64,32]{1,2,0:T(8,128)(2,1)S(1)} %get-tuple-element.20, bf16[16,64,32]{1,2,0:T(8,128)(2,1)S(1)} %get-tuple-element.19, bf16[16,64,32]{1,2,0:T(8,128)(2,1)S(1)} %fusion.46), kind=kOutput, calls=%fused_computation.55 | convolution fusion | flops 269484032 | bytes 10682368 | tf_op jit(solution)/shard_map/pjk,pkr->pjr/dot_general | solution.py:44
  70.0 2.1 %multiply_subtract_fusion.1 = (f32[16,1,64,1024]{3,2,1,0:T(8,128)S(1)}, f32[16,1,64,1024]{3,2,1,0:T(8,128)S(1)}) fusion(f32[16,2,64,1024]{3,2,1,0:T(8,128)S(1)} %bitcast.135, f32[16,1024]{1,0:T(8,128)S(1)} %get-tuple-element.37, f32[16,1024]{1,0:T(8,128)S(1)} %get-tuple-element.38), kind=kLoop, calls=%fused_computation.28 | loop fusion | flops 6291456 | bytes 16908288 | tf_op jit(solution)/shard_map/sub | solution.py:53
  72.0 1.1 %fusion.4 = (f32[4,1,2,2,2,32,1024]{6,5,4,2,1,0,3:T(8,128)S(1)}, f32[4,1,2,2,2,32,1024]{6,5,4,2,1,0,3:T(8,128)S(1)}) fusion(f32[4,2,2,1,2,32,1024]{6,5,4,2,1,0,3:T(8,128)S(1)} %bitcast.141, f32[4,2,2,1,2,32,1024]{6,5,4,2,1,0,3:T(8,128)S(1)} %bitcast.142), kind=kLoop, calls=%fused_computation.11 | loop fusion | flops 2097152 | bytes 16777216 | tf_op jit(solution)/shard_map/stack | solution.py:55
  73.2 1.1 %fusion.7 = bf16[4,1,2,2,2,32,1024]{6,5,3,2,4,0,1:T(8,128)(2,1)S(1)} fusion(f32[4,1,2,2,2,32,1024]{6,5,4,2,1,0,3:T(8,128)S(1)} %get-tuple-element.14, f32[4,1,2,2,2,32,1024]{6,5,4,2,1,0,3:T(8,128)S(1)} %get-tuple-element.13), kind=kLoop, calls=%fused_computation.20 | loop fusion | flops 3145728 | bytes 10485760 | tf_op jit(solution)/shard_map/convert_element_type | solution.py:58
  74.3 1.7 %fusion.12 = f32[16,128,1024]{2,1,0:T(8,128)S(1)} fusion(bf16[16,64,1024]{2,1,0:T(8,128)(2,1)S(1)} %bitcast.144, bf16[16,64,32]{1,2,0:T(8,128)(2,1)S(1)} %get-tuple-element.18, bf16[16,64,32]{1,2,0:T(8,128)(2,1)S(1)} %get-tuple-element.17, bf16[16,64,32]{1,2,0:T(8,128)(2,1)S(1)} %fusion.45), kind=kOutput, calls=%fused_computation.47 | convolution fusion | flops 269484032 | bytes 10682368 | tf_op jit(solution)/shard_map/pjk,pkr->pjr/dot_general | solution.py:44
  76.1 2.1 %multiply_subtract_fusion = (f32[16,1,64,1024]{3,2,0,1:T(8,128)S(1)}, f32[16,1,64,1024]{3,2,0,1:T(8,128)S(1)}) fusion(f32[16,2,64,1024]{3,2,1,0:T(8,128)S(1)} %bitcast.133, f32[16,1024]{1,0:T(8,128)S(1)} %get-tuple-element.32, f32[16,1024]{1,0:T(8,128)S(1)} %get-tuple-element.31), kind=kLoop, calls=%fused_computation.26 | loop fusion | flops 6291456 | bytes 16908288 | tf_op jit(solution)/shard_map/sub | solution.py:53
  78.1 1.0 %convert_bitcast_fusion = f32[2,2,4,2,32,1024]{5,4,1,2,0,3:T(8,128)S(1)} fusion(f32[2,2,4,1,2,32,1024]{6,5,4,2,1,0,3:T(8,128)S(1)} %bitcast.138, f32[2,2,4,1,2,32,1024]{6,5,4,2,1,0,3:T(8,128)S(1)} %bitcast.137), kind=kLoop, calls=%fused_computation.24 | loop fusion | flops 6291456 | bytes 12582912 | tf_op jit(solution)/shard_map/convert_element_type | solution.py:60
  79.7 0.7 subtract_reduce_fusion
  80.7 1.5 %copy.64 = bf16[1,2,32,8,1024]{4,3,2,1,0:T(8,128)(2,1)} copy(bf16[1,2,32,8,1024]{4,2,3,1,0:T(8,128)(2,1)S(1)} %fusion.11) | data formatting | bytes 2097152 | tf_op jit(solution)/shard_map/convert_element_type | solution.py:66
  (37 shorter events, 2.9 us)
Async XLA Ops:
  6.4 9.9 %copy-start.5 = (f32[3,16,2]{1,2,0:T(2,128)S(1)}, f32[3,16,2]{1,2,0:T(2,128)}, u32[]{:S(2)}) copy-start(f32[3,16,2]{1,2,0:T(2,128)} %param.11) | copy-start | bytes 1156
  6.4 9.9 %copy-start.6 = (s32[16]{0:T(128)S(1)}, s32[16]{0:T(128)}, u32[]{:S(2)}) copy-start(s32[16]{0:T(128)} %param.12) | copy-start | bytes 196
  6.4 11.2 %copy-start.3 = (s32[3,16,64]{2,1,0:T(8,128)S(1)}, s32[3,16,64]{2,1,0:T(8,128)}, u32[]{:S(2)}) copy-start(s32[3,16,64]{2,1,0:T(8,128)} %param.10) | copy-start | bytes 36868
  6.4 11.2 %copy-start.4 = (f32[1,2,1024]{2,1,0:T(2,128)S(1)}, f32[1,2,1024]{2,1,0:T(2,128)}, u32[]{:S(2)}) copy-start(f32[1,2,1024]{2,1,0:T(2,128)} %param.13) | copy-start | bytes 24580
  6.4 11.4 %copy-start.2 = (bf16[3,16,2,64,8]{3,4,2,1,0:T(8,128)(2,1)S(1)}, bf16[3,16,2,64,8]{3,4,2,1,0:T(8,128)(2,1)}, u32[]{:S(2)}) copy-start(bf16[3,16,2,64,8]{3,4,2,1,0:T(8,128)(2,1)} %param.9) | copy-start | bytes 294916
  9.7 52.6 %all-to-all-start = ((bf16[16,2,32,1024]{3,2,1,0:T(8,128)(2,1)}), bf16[16,2,32,1024]{3,2,1,0:T(8,128)(2,1)S(1)}, u32[]{:S(2)}, u32[]{:S(2)}) async-start(bf16[16,2,32,1024]{3,2,1,0:T(8,128)(2,1)} %broadcast_select_fusion), calls=%async_computation | async-start | bytes 4194304 | tf_op jit(solution)/shard_map/all_to_all | solution.py:39
  62.3 1.8 %copy-start = (f32[16,1024]{1,0:T(8,128)S(1)}, f32[16,1024]{1,0:T(8,128)}, u32[]{:S(2)}) copy-start(f32[16,1024]{1,0:T(8,128)} %get-tuple-element.39) | copy-start | bytes 196612
  62.3 1.8 %copy-start.1 = (f32[16,1024]{1,0:T(8,128)S(1)}, f32[16,1024]{1,0:T(8,128)}, u32[]{:S(2)}) copy-start(f32[16,1024]{1,0:T(8,128)} %get-tuple-element.40) | copy-start | bytes 196612

commit v2 on v1

v2 whole, which is shorter than its diff:
```python
import functools

import jax
import jax.numpy as jnp
from jax import lax
from jax.experimental import pallas as pl
from jax.experimental.pallas import tpu as pltpu
from jax.sharding import PartitionSpec as P

SECTIONS = 3
SECTORS = 2**SECTIONS
HALF_ROOT = 0.7071067811865476
LANES = 128
MESH = pl.DeviceIdType.MESH


def fill_operators(count, weights, starts_ref, operators):
    beams = operators.shape[2] // 4
    taps = weights.shape[3]
    beam = lax.broadcasted_iota(jnp.int32, (beams, 4 * beams), 0)

    for level in range(SECTIONS):
        step = 1 << level

        def pair(i, carry, level=level, step=step):
            low = (i // step) * (2 * step) + i % step
            columns = []
            for p in (low, low + step):
                starts = starts_ref[level, pl.ds(p, 1), :]
                offset = beam - jnp.concatenate([starts, starts], axis=1)
                real = weights[level, p, 0].astype(jnp.float32)
                imag = weights[level, p, 1].astype(jnp.float32)
                for both in ((real, imag), (-imag, real)):
                    taps_of = jnp.concatenate(both, axis=1)
                    dense = jnp.zeros(beam.shape, jnp.float32)
                    for t in range(taps):
                        dense = jnp.where(offset == t, taps_of[t : t + 1], dense)
                    columns.append(dense)
            stacked = jnp.concatenate(columns, axis=0)
            operators[level, i] = jnp.transpose(stacked).astype(jnp.bfloat16)
            return carry

        lax.fori_loop(0, count // 2, pair, 0)


def on_rows(row):
    size = row.shape[1]
    diagonal = lax.broadcasted_iota(jnp.int32, (size, size), 0) == lax.broadcasted_iota(
        jnp.int32, (size, size), 1
    )
    return jnp.sum(jnp.where(diagonal, row, 0.0), axis=1, keepdims=True)


def kernel(
    count,
    width,
    range_count,
    owner_ref,
    shift_ref,
    sub_ref,
    weights_ref,
    starts_ref,
    params_ref,
    group_ref,
    out_ref,
    local,
    columns,
    outgoing,
    incoming,
    weights,
    operators,
    cosines,
    sines,
    group_cosines,
    group_sines,
    total,
    staged,
    load_sem,
    weight_sem,
    out_sem,
    send_sem,
    recv_sem,
):
    me = lax.axis_index("aperture")
    half = count // 2
    side = me // half
    place = me % half
    block = range_count // count
    chunks = block // width
    groups = count // SECTORS
    rows = local.shape[0]
    beams = rows // 2

    load = pltpu.make_async_copy(sub_ref, local, load_sem)
    load.start()
    weight_load = pltpu.make_async_copy(weights_ref, weights, weight_sem)
    weight_load.start()
    barrier = pltpu.get_barrier_semaphore()

    def greet(j, carry):
        pl.semaphore_signal(
            barrier, inc=1, device_id={"aperture": (me + j) % count}, device_id_type=MESH
        )
        return carry

    lax.fori_loop(1, count, greet, 0)
    columns[0] = jnp.zeros((rows, LANES), jnp.bfloat16)
    load.wait()

    def split(k, carry):
        for v in range(8):
            at = k * 8 + v
            columns[at + 1] = local[:, pl.ds(pl.multiple_of(at * LANES, LANES), LANES)]
        return carry

    lax.fori_loop(0, range_count // LANES // 8, split, 0)
    pl.semaphore_wait(barrier, count - 1)

    reach = 2 * LANES
    source_bin = lax.broadcasted_iota(jnp.int32, (reach, LANES), 0)
    target_bin = lax.broadcasted_iota(jnp.int32, (reach, LANES), 1)
    move = (source_bin == target_bin + LANES - shift_ref[...]).astype(jnp.bfloat16)

    def shifted(to, c):
        first = owner_ref[to] * (block // LANES) + c * (width // LANES)
        tiles = [columns[first + v] for v in range(width // LANES + 1)]
        windows = [jnp.concatenate(tiles[v : v + 2], axis=1) for v in range(width // LANES)]
        moved = jnp.dot(
            jnp.concatenate(windows, axis=0), move, preferred_element_type=jnp.float32
        ).astype(jnp.bfloat16)
        return jnp.concatenate(
            [moved[v * rows : (v + 1) * rows] for v in range(width // LANES)], axis=1
        )

    def transfer(to, c):
        return pltpu.make_async_remote_copy(
            src_ref=outgoing.at[c, to],
            dst_ref=incoming.at[c, me],
            send_sem=send_sem.at[c, to],
            recv_sem=recv_sem.at[c, me],
            device_id={"aperture": to},
            device_id_type=MESH,
        )

    def send(to, c):
        outgoing[c, to] = shifted(to, c)
        transfer(to, c).start()

    def far(j):
        return (1 - side) * half + (place + j) % half

    def near(j):
        return side * half + (place + j) % half

    def send_chunk(c, carry):
        send(far(0), c)

        def both(j, carry):
            send(far(j), c)
            send(near(j), c)
            return carry

        lax.fori_loop(1, half, both, 0)
        return carry

    lax.fori_loop(0, chunks, send_chunk, 0)

    def keep_chunk(c, carry):
        incoming[c, me] = shifted(me, c)
        return carry

    lax.fori_loop(0, chunks, keep_chunk, 0)

    first = owner_ref[me] * block
    position = (first + lax.broadcasted_iota(jnp.int32, (1, block), 1)).astype(
        jnp.float32
    ) / range_count
    for level in range(SECTIONS):
        params = params_ref[level]
        angle = on_rows(params[0:1]) * position + on_rows(params[1:2])
        cosines[level] = jnp.cos(angle)
        sines[level] = jnp.sin(angle)
    scale = HALF_ROOT**SECTIONS / groups**0.5
    group_cosines[...] = jnp.cos(group_ref[...]) * scale
    group_sines[...] = jnp.sin(group_ref[...]) * scale
    weight_load.wait()
    fill_operators(count, weights, starts_ref, operators)

    def arrived(source, c):
        @pl.when(source != me)
        def _():
            pltpu.make_async_remote_copy(
                src_ref=outgoing.at[c, source],
                dst_ref=incoming.at[c, source],
                send_sem=send_sem.at[c, source],
                recv_sem=recv_sem.at[c, source],
                device_id={"aperture": source},
                device_id_type=MESH,
            ).wait_recv()

    def merge(g, c, is_first):
        def wait_one(s, carry):
            arrived(g * SECTORS + s, c)
            return carry

        lax.fori_loop(0, SECTORS, wait_one, 0)
        bins = pl.ds(pl.multiple_of(c * width, LANES), width)
        images = []
        for s in range(SECTORS):
            whole = incoming[c, g * SECTORS + s].astype(jnp.float32)
            images.append((whole[0:beams], whole[beams:rows]))

        def turned(image, cosine, sine):
            real, imag = image
            return real * cosine - imag * sine, real * sine + imag * cosine

        for level in range(SECTIONS):
            step = 1 << level
            merged = [None] * SECTORS
            for i in range(SECTORS // 2):
                low = (i // step) * (2 * step) + i % step
                high = low + step
                parts = []
                for s in (low, high):
                    row = pl.ds(g * SECTORS + s, 1)
                    parts += turned(images[s], cosines[level, row, bins], sines[level, row, bins])
                stacked = jnp.concatenate([part.astype(jnp.bfloat16) for part in parts], axis=0)
                product = jnp.dot(
                    operators[level, g * (SECTORS // 2) + i],
                    stacked,
                    preferred_element_type=jnp.float32,
                )
                merged[low] = (product[0:beams], product[rows : rows + beams])
                merged[high] = (product[beams:rows], product[rows + beams : 2 * rows])
            images = merged
        for s in range(SECTORS):
            row = pl.ds(g, 1)
            pieces = turned(images[s], group_cosines[row, bins], group_sines[row, bins])
            for part in range(2):
                at = pl.ds(part * beams * SECTORS + s, beams, stride=SECTORS)
                for v in range(width // LANES):
                    tile = pieces[part][:, v * LANES : (v + 1) * LANES]
                    tile_at = c * (width // LANES) + v
                    if is_first:
                        total[tile_at, at, :] = tile
                    else:
                        total[tile_at, at, :] += tile

    own = me // SECTORS

    def own_chunk(c, carry):
        merge(own, c, True)
        return carry

    lax.fori_loop(0, chunks, own_chunk, 0)

    def write(c):
        return pltpu.make_async_copy(
            staged.at[c],
            out_ref.at[:, pl.ds(pl.multiple_of(c * width, LANES), width)],
            out_sem.at[c],
        )

    def other_chunk(c, carry):
        def other_group(k, carry):
            merge((own + k) % groups, c, False)
            return carry

        lax.fori_loop(1, groups, other_group, 0)
        for v in range(width // LANES):
            staged[c, :, v * LANES : (v + 1) * LANES] = total[
                c * (width // LANES) + v
            ].astype(jnp.bfloat16)
        write(c).start()
        return carry

    lax.fori_loop(0, chunks, other_chunk, 0)

    def finish(c, carry):
        write(c).wait()

        def sent(j, carry):
            transfer((me + j) % count, c).wait_send()
            return carry

        lax.fori_loop(1, count, sent, 0)
        return carry

    lax.fori_loop(0, chunks, finish, 0)


def shards(
    subimages, range_shift, interp_weights, band_start, phase_params, block_owner, group_phase
):
    beams, range_count = subimages.shape[2:]
    count = lax.axis_size("aperture")
    block = range_count // count
    width = min(256, block)
    chunks = block // width
    groups = count // SECTORS
    rows = 2 * beams
    bf16, f32 = jnp.bfloat16, jnp.float32
    taps_first = jnp.swapaxes(interp_weights, 3, 4)
    anywhere = pl.BlockSpec(memory_space=pl.ANY)
    scalars = pl.BlockSpec(memory_space=pltpu.SMEM)
    vectors = pl.BlockSpec(memory_space=pltpu.VMEM)
    combined = pl.pallas_call(
        functools.partial(kernel, count, width, range_count),
        out_shape=jax.ShapeDtypeStruct((rows * SECTORS, block), bf16),
        in_specs=[scalars, vectors, anywhere, anywhere, vectors, vectors, vectors],
        out_specs=anywhere,
        scratch_shapes=[
            pltpu.VMEM((rows, range_count), bf16),
            pltpu.VMEM((range_count // LANES + 1, rows, LANES), bf16),
            pltpu.VMEM((chunks, count, rows, width), bf16),
            pltpu.VMEM((chunks, count, rows, width), bf16),
            pltpu.VMEM(taps_first.shape, bf16),
            pltpu.VMEM((SECTIONS, count // 2, 2 * rows, 2 * rows), bf16),
            pltpu.VMEM((SECTIONS, count, block), f32),
            pltpu.VMEM((SECTIONS, count, block), f32),
            pltpu.VMEM((groups, block), f32),
            pltpu.VMEM((groups, block), f32),
            pltpu.VMEM((block // LANES, rows * SECTORS, LANES), f32),
            pltpu.VMEM((chunks, rows * SECTORS, width), bf16),
            pltpu.SemaphoreType.DMA,
            pltpu.SemaphoreType.DMA,
            pltpu.SemaphoreType.DMA((chunks,)),
            pltpu.SemaphoreType.DMA((chunks, count)),
            pltpu.SemaphoreType.DMA((chunks, count)),
        ],
        compiler_params=pltpu.CompilerParams(
            collective_id=0, has_side_effects=True, vmem_limit_bytes=56 * 1024 * 1024
        ),
        cost_estimate=pl.CostEstimate(
            flops=SECTIONS * 4 * rows * rows * range_count,
            bytes_accessed=3 * rows * range_count,
            transcendentals=2 * (SECTIONS * count + groups) * block,
        ),
    )(
        block_owner,
        range_shift.reshape(1, 1),
        subimages.reshape(rows, range_count),
        taps_first,
        band_start,
        jnp.swapaxes(phase_params, 1, 2),
        group_phase[0],
    )
    return combined.reshape(1, 2, beams, SECTORS, block)


def solution(mesh):
    placed = (
        P(("scene", "aperture"), None, None, None),
        P(("scene", "aperture")),
        P(None, "scene", None, None, None),
        P(None, "scene", None),
        P(None, "scene", None),
        P("scene"),
        P(("scene", "aperture"), None, None),
    )
    return jax.shard_map(
        shards,
        mesh=mesh,
        in_specs=placed,
        out_specs=P(("scene", "aperture"), None, None, None, None),
        check_vma=False,
    )
```

time: 83.9 us -> 59.5 us (0.71)
  the two profiles are of different devices: /device:TPU:9 before, /device:TPU:0 now
where the time goes in v2:
time: 59.5 us; the launch traced here: 59.2 us
  Pallas kernels  56.3 us (95%)
  local copies, waits for them, and re-layouts  2.26 us (4%)
  between operations  0.66 us (1%)
    pallas_call x1, Pallas kernels, shards(): pl.pallas_call(functools.partial(kernel, count, width, range_count), out_...  56.3 us
    unnamed x1, local copies, waits for them, and re-layouts  2.26 us

profile of v2, /device:TPU:0, one launch (start us, length us, event | category | flops | bytes accessed | tf_op | source)
XLA Modules:
  0.0 59.2 jit_solution(10391892261327408178)
XLA Ops:
  0.7 56.3 %shard_map.73 = bf16[512,1024]{1,0:T(8,128)(2,1)} custom-call(s32[16]{0:T(128)} %owner_ref.1, s32[1,1]{1,0:T(1,128)} %bitcast.6.shift_ref, bf16[64,16384]{1,0:T(8,128)(2,1)} %bitcast.8, bf16[3,16,2,8,64]{4,3,2,1,0:T(8,128)(2,1)} %bitcast.9, s32[3,16,64]{2,1,0:T(8,128)} %starts_ref.1, f32[3,2,16]{2,1,0:T(2,128)} %bitcast.11, f32[2,1024]{1,0:T(2,128)} %bitcast.10), custom_call_target="tpu_custom_call" | custom-call | flops 805306368 | bytes 3145728 | tf_op jit(solution)/shard_map/pallas_call | solution.py:307
  57.0 2.3 %copy.10 = bf16[1,2,32,8,1024]{4,3,2,1,0:T(8,128)(2,1)} copy(bf16[1,2,32,8,1024]{4,3,2,1,0:T(8,128)(2,1)} %bitcast.7) | data formatting | bytes 2097152

commit v3 on v2

--- a/solution.py
+++ b/solution.py
@@ -91,8 +91,15 @@
     rows = local.shape[0]
     beams = rows // 2
 
-    load = pltpu.make_async_copy(sub_ref, local, load_sem)
-    load.start()
+    pieces = load_sem.shape[0]
+    piece = range_count // pieces
+
+    def load(k):
+        bins = pl.ds(k * piece, piece)
+        return pltpu.make_async_copy(sub_ref.at[:, bins], local.at[:, bins], load_sem.at[k])
+
+    for k in range(pieces):
+        load(k).start()
     weight_load = pltpu.make_async_copy(weights_ref, weights, weight_sem)
     weight_load.start()
     barrier = pltpu.get_barrier_semaphore()
@@ -105,15 +112,16 @@
 
     lax.fori_loop(1, count, greet, 0)
     columns[0] = jnp.zeros((rows, LANES), jnp.bfloat16)
-    load.wait()
-
-    def split(k, carry):
-        for v in range(8):
-            at = k * 8 + v
-            columns[at + 1] = local[:, pl.ds(pl.multiple_of(at * LANES, LANES), LANES)]
-        return carry
-
-    lax.fori_loop(0, range_count // LANES // 8, split, 0)
+    for k in range(pieces):
+        load(k).wait()
+
+        def split(i, carry, k=k):
+            for v in range(8):
+                at = k * (piece // LANES) + i * 8 + v
+                columns[at + 1] = local[:, pl.ds(pl.multiple_of(at * LANES, LANES), LANES)]
+            return carry
+
+        lax.fori_loop(0, piece // LANES // 8, split, 0)
     pl.semaphore_wait(barrier, count - 1)
 
     reach = 2 * LANES
@@ -136,7 +144,7 @@
         return pltpu.make_async_remote_copy(
             src_ref=outgoing.at[c, to],
             dst_ref=incoming.at[c, me],
-            send_sem=send_sem.at[c, to],
+            send_sem=send_sem,
             recv_sem=recv_sem.at[c, me],
             device_id={"aperture": to},
             device_id_type=MESH,
@@ -146,24 +154,41 @@
         outgoing[c, to] = shifted(to, c)
         transfer(to, c).start()
 
-    def far(j):
-        return (1 - side) * half + (place + j) % half
+    quarter = count // 4
+    corner = me % quarter
+
+    def outer(j):
+        return (1 - side) * 3 * quarter + (corner + j) % quarter
+
+    def inner(j):
+        return (2 - side) * quarter + (corner + j) % quarter
 
     def near(j):
         return side * half + (place + j) % half
 
-    def send_chunk(c, carry):
-        send(far(0), c)
-
-        def both(j, carry):
-            send(far(j), c)
-            send(near(j), c)
-            return carry
-
-        lax.fori_loop(1, half, both, 0)
-        return carry
-
-    lax.fori_loop(0, chunks, send_chunk, 0)
+    def send_first(c, carry):
+        def three(j, carry):
+            send(outer(j), c)
+            send(near(2 * j + 1), c)
+            send(near(2 * j + 2), c)
+            return carry
+
+        lax.fori_loop(0, quarter - 1, three, 0)
+        send(outer(quarter - 1), c)
+        send(near(half - 1), c)
+        return carry
+
+    lax.fori_loop(0, chunks, send_first, 0)
+
+    def send_second(c, carry):
+        def one(j, carry):
+            send(inner(j), c)
+            return carry
+
+        lax.fori_loop(0, quarter, one, 0)
+        return carry
+
+    lax.fori_loop(0, chunks, send_second, 0)
 
     def keep_chunk(c, carry):
         incoming[c, me] = shifted(me, c)
@@ -192,7 +217,7 @@
             pltpu.make_async_remote_copy(
                 src_ref=outgoing.at[c, source],
                 dst_ref=incoming.at[c, source],
-                send_sem=send_sem.at[c, source],
+                send_sem=send_sem,
                 recv_sem=recv_sem.at[c, source],
                 device_id={"aperture": source},
                 device_id_type=MESH,
@@ -278,15 +303,11 @@
 
     def finish(c, carry):
         write(c).wait()
-
-        def sent(j, carry):
-            transfer((me + j) % count, c).wait_send()
-            return carry
-
-        lax.fori_loop(1, count, sent, 0)
         return carry
 
     lax.fori_loop(0, chunks, finish, 0)
+    every = outgoing.at[:, pl.ds(0, count - 1)]
+    pltpu.make_async_copy(every, every, send_sem).wait()
 
 
 def shards(
@@ -322,10 +343,10 @@
             pltpu.VMEM((groups, block), f32),
             pltpu.VMEM((block // LANES, rows * SECTORS, LANES), f32),
             pltpu.VMEM((chunks, rows * SECTORS, width), bf16),
-            pltpu.SemaphoreType.DMA,
+            pltpu.SemaphoreType.DMA((4,)),
             pltpu.SemaphoreType.DMA,
             pltpu.SemaphoreType.DMA((chunks,)),
-            pltpu.SemaphoreType.DMA((chunks, count)),
+            pltpu.SemaphoreType.DMA,
             pltpu.SemaphoreType.DMA((chunks, count)),
         ],
         compiler_params=pltpu.CompilerParams(

time: 59.5 us -> 56.7 us (0.953)
  the two profiles are of different devices: /device:TPU:0 before, /device:TPU:9 now
where the time goes in v3:
time: 56.7 us; the launch traced here: 56.5 us
  Pallas kernels  53.6 us (95%)
  local copies, waits for them, and re-layouts  2.26 us (4%)
  between operations  0.66 us (1%)
    pallas_call x1, Pallas kernels, shards(): pl.pallas_call(functools.partial(kernel, count, width, range_count), out_...  53.6 us
    unnamed x1, local copies, waits for them, and re-layouts  2.26 us

profile of v3, /device:TPU:9, one launch (start us, length us, event | category | flops | bytes accessed | tf_op | source)
XLA Modules:
  0.0 56.5 jit_solution(13314163309667598255)
XLA Ops:
  0.7 53.6 %shard_map.73 = bf16[512,1024]{1,0:T(8,128)(2,1)} custom-call(s32[16]{0:T(128)} %owner_ref.1, s32[1,1]{1,0:T(1,128)} %bitcast.6.shift_ref, bf16[64,16384]{1,0:T(8,128)(2,1)} %bitcast.8, bf16[3,16,2,8,64]{4,3,2,1,0:T(8,128)(2,1)} %bitcast.9, s32[3,16,64]{2,1,0:T(8,128)} %starts_ref.1, f32[3,2,16]{2,1,0:T(2,128)} %bitcast.11, f32[2,1024]{1,0:T(2,128)} %bitcast.10), custom_call_target="tpu_custom_call" | custom-call | flops 805306368 | bytes 3145728 | tf_op jit(solution)/shard_map/pallas_call | solution.py:328
  54.2 2.3 %copy.10 = bf16[1,2,32,8,1024]{4,3,2,1,0:T(8,128)(2,1)} copy(bf16[1,2,32,8,1024]{4,3,2,1,0:T(8,128)(2,1)} %bitcast.7) | data formatting | bytes 2097152

commit v4 on v3

--- a/solution.py
+++ b/solution.py
@@ -308,6 +308,25 @@
     lax.fori_loop(0, chunks, finish, 0)
     every = outgoing.at[:, pl.ds(0, count - 1)]
     pltpu.make_async_copy(every, every, send_sem).wait()
+
+
+def hand_over(from_ref, out_ref, held, in_sems, out_sems):
+    size = held.shape[1]
+    pieces = held.shape[0]
+
+    def bring(k):
+        return pltpu.make_async_copy(from_ref.at[pl.ds(k * size, size)], held.at[k], in_sems.at[k])
+
+    def put(k):
+        return pltpu.make_async_copy(held.at[k], out_ref.at[pl.ds(k * size, size)], out_sems.at[k])
+
+    for k in range(pieces):
+        bring(k).start()
+    for k in range(pieces):
+        bring(k).wait()
+        put(k).start()
+    for k in range(pieces):
+        put(k).wait()
 
 
 def shards(
@@ -366,6 +385,18 @@
         jnp.swapaxes(phase_params, 1, 2),
         group_phase[0],
     )
+    combined = pl.pallas_call(
+        hand_over,
+        out_shape=jax.ShapeDtypeStruct(combined.shape, bf16),
+        in_specs=[anywhere],
+        out_specs=anywhere,
+        scratch_shapes=[
+            pltpu.VMEM((4, rows * SECTORS // 4, block), bf16),
+            pltpu.SemaphoreType.DMA((4,)),
+            pltpu.SemaphoreType.DMA((4,)),
+        ],
+        compiler_params=pltpu.CompilerParams(vmem_limit_bytes=56 * 1024 * 1024),
+    )(combined)
     return combined.reshape(1, 2, beams, SECTORS, block)
 
 

time: 56.7 us -> 56.4 us (level)
  local copies, waits for them, and re-layouts: 2.26 us -> 0 us
  Pallas kernels: 53.6 us -> 55.5 us
    unnamed x1 -> x0, local copies, waits for them, and re-layouts: 2.26 us -> none
    pallas_call x0 -> x1, Pallas kernels: none -> 1.98 us  [shards(): pl.pallas_call(hand_over, out_shape=jax.ShapeDtypeStruct(combined.shape,...]
where the time goes in v4:
time: 56.4 us; the launch traced here: 56.2 us
  Pallas kernels  55.5 us (98%)
  between operations  0.66 us (1%)
    pallas_call x1, Pallas kernels, shards(): pl.pallas_call(functools.partial(kernel, count, width, range_count), out_...  53.6 us
    pallas_call x1, Pallas kernels, shards(): pl.pallas_call(hand_over, out_shape=jax.ShapeDtypeStruct(combined.shape,...  1.98 us

profile of v4, /device:TPU:9, one launch (start us, length us, event | category | flops | bytes accessed | tf_op | source)
XLA Modules:
  0.0 56.2 jit_solution(15701705766613927131)
XLA Ops:
  0.7 53.6 %shard_map.73.from_ref = bf16[512,1024]{1,0:T(8,128)(2,1)} custom-call(s32[16]{0:T(128)} %owner_ref.1, s32[1,1]{1,0:T(1,128)} %bitcast.6.shift_ref, bf16[64,16384]{1,0:T(8,128)(2,1)} %bitcast.7, bf16[3,16,2,8,64]{4,3,2,1,0:T(8,128)(2,1)} %bitcast.8, s32[3,16,64]{2,1,0:T(8,128)} %starts_ref.1, f32[3,2,16]{2,1,0:T(2,128)} %bitcast.10, f32[2,1024]{1,0:T(2,128)} %bitcast.9), custom_call_target="tpu_custom_call" | custom-call | flops 805306368 | bytes 3145728 | tf_op jit(solution)/shard_map/pallas_call | solution.py:347
  54.2 2.0 %shard_map.74 = bf16[512,1024]{1,0:T(8,128)(2,1)} custom-call(bf16[512,1024]{1,0:T(8,128)(2,1)} %shard_map.73.from_ref), custom_call_target="tpu_custom_call" | custom-call | tf_op jit(solution)/shard_map/pallas_call | solution.py:388
